TPU v7x, 128 devices: a whole 4x4x4 slice. The times are simulated.
128 devices in a mesh: dp: 32 (over z, y, core), tp: 4 (over x).
Axes of the slice: x: 4, y: 4, z: 4, core: 2. Of those that a mesh axis runs over, the one named last changes fastest.
Arguments:
- hidden_in: bfloat16 [64, 512, 768], P('dp', 'tp'), may hold values from -6 to 6
- reset: int32 [64], P('dp'), may hold values from 0 to 1, as said below
- w_qkv: bfloat16 [768, 2304], P(('dp', 'tp')), may hold values from -0.21875 to 0.21875
- w_attn_out: bfloat16 [768, 768], P(('dp', 'tp')), may hold values from -0.3125 to 0.3125
- norm_gains: bfloat16 [2, 768], P(None, ('dp', 'tp')), may hold values from 0.5 to 1.5
- norm_biases: bfloat16 [2, 768], P(None, ('dp', 'tp')), may hold values from -2 to 2
- memory_tokens: bfloat16 [2, 10, 768], P(None, None, ('dp', 'tp')), may hold values from -6 to 6
- w_in: bfloat16 [768, 3072], P('dp', 'tp'), may hold values from -0.21875 to 0.21875
- w_out: bfloat16 [3072, 768], P('tp', 'dp'), may hold values from -0.109375 to 0.109375
- grad_hidden: bfloat16 [64, 512, 768], P('dp', 'tp'), may hold values from -6 to 6
- grad_memory: bfloat16 [64, 20, 768], P('dp', 'tp'), may hold values from -6 to 6
Outputs:
- hidden_out: bfloat16 [64, 512, 768], P('dp', 'tp')
- memory_out: bfloat16 [64, 20, 768], P('dp', 'tp')
- grad_in: float32 [64, 512, 768], P('dp', 'tp')
- grad_qkv: float32 [768, 2304], P(('dp', 'tp'))
- grad_attn_out: float32 [768, 768], P(('dp', 'tp'))
- grad_gains: float32 [2, 768], P(None, ('dp', 'tp'))
- grad_biases: float32 [2, 768], P(None, ('dp', 'tp'))
- grad_memory_tokens: float32 [2, 10, 768], P(None, None, ('dp', 'tp'))
- grad_w_in: float32 [768, 3072], P('dp', 'tp')
- grad_w_out: float32 [3072, 768], P('tp', 'dp')
Inputs may be any that keep to these rules, and one draw needn't show every extreme that they name: reset is 1 at the first segment of every index of dp; each index of dp holds one chain of exactly 2 segments: reset is 1 at its first segment and 0 at its second.
All inputs are finite; a program needn't handle non-finite values.
Results may differ from a plain program's by a relative error of at most 0.017.
Values may be sent and summed in bfloat16 or wider, within the bound.
A program may use at most 128 MiB of HBM per device.

v0:
```python
import functools
import types

import jax
import jax.numpy as jnp
import numpy as np
from jax import lax
from jax.experimental import pallas as pl
from jax.experimental.pallas import tpu as pltpu
from jax.sharding import PartitionSpec as P

D = 768
HALF = 384
MEM = 10
TOKENS = 64
OWN = 272
ROWS = 2 * OWN
TP = 4
SMALL = 128
ACOLS = 4 * HALF + SMALL
REST = ACOLS - HALF
CUT = HALF + 640
WO = 3 * HALF
EPSILON = 1e-05
INV_ROOT_TWO = 0.7071067811865476
INV_ROOT_TWOPI = 0.3989422804014327
EXP_SCALE = 0.125 * 1.4426950408889634
MASKED = -1e30
F32 = jnp.float32
BF16 = jnp.bfloat16
MESH = pl.DeviceIdType.MESH
NN = (((1,), (0,)), ((), ()))
NT = (((1,), (1,)), ((), ()))
TN = (((0,), (0,)), ((), ()))


def dot(a, b, dims=NN):
    return lax.dot_general(a, b, dims, preferred_element_type=F32)


def up16(n):
    return -(-n // 16) * 16


class Shape:
    def __init__(self, dp):
        self.dp = dp
        planes = dp // 2
        self.ny = int(round(planes**0.5))
        self.nz = planes // self.ny
        self.wrows = D // dp
        self.arows = D // (dp * TP)
        self.brows = 2 * self.wrows
        self.pr = up16(self.arows)
        self.xrows = 2 * self.arows * self.ny
        self.pc = -(-self.arows // 8) * 8
        self.fr = up16(self.wrows)


def selections(sh):
    pack = np.zeros((sh.brows, TP * 2 * sh.pc), np.float32)
    for c in range(2):
        for x in range(TP):
            for i in range(sh.arows):
                pack[c * sh.wrows + x * sh.arows + i, (x * 2 + c) * sh.pc + i] = 1
    packy = np.zeros((sh.xrows, sh.ny * 2 * sh.pc), np.float32)
    turn = np.zeros((D, D), np.float32)
    ar = sh.arows
    for c in range(2):
        for y in range(sh.ny):
            for i in range(ar):
                row = (y * 2 + c) * ar + i
                packy[row, (y * 2 + c) * sh.pc + i] = 1
                for x in range(TP):
                    for z in range(sh.nz):
                        place = (z * sh.ny + y) * sh.brows + (c * TP + x) * ar + i
                        turn[(x * sh.nz + z) * sh.xrows + row, place] = 1
    small = np.zeros((48, SMALL), np.float32)
    for i in range(4):
        small[i, i] = 1
    for kind in range(2):
        for i in range(MEM):
            small[16 + 16 * kind + (i // 5) * 8 + i % 5, 4 + MEM * kind + i] = 1
    places = np.zeros((4, MEM, SMALL), np.float32)
    for kind, (rows, first) in enumerate(((2, 0), (2, 2), (MEM, 4), (MEM, 4 + MEM))):
        for i in range(rows):
            places[kind, i, first + i] = 1
    return pack, small, places, packy, turn


def norm_forward(inputs, gain, offset):
    centred = inputs - jnp.mean(inputs, -1, keepdims=True)
    spread = jnp.mean(centred * centred, -1, keepdims=True)
    inverse = lax.rsqrt(spread + EPSILON)
    normed = centred * inverse
    return normed * gain + offset, normed, inverse


def norm_backward(upstream, normed, inverse, gain):
    scaled = upstream * gain
    first_mean = jnp.mean(scaled, -1, keepdims=True)
    second_mean = jnp.mean(scaled * normed, -1, keepdims=True)
    return inverse * (scaled - first_mean - normed * second_mean)


def column_sum(a):
    return jnp.sum(a, 0, keepdims=True)


XBASE = (0, 4, 8, 10, 14, 16, 20)
SENDS = 40
STAGED, LANDED, SUMMED, PASSED, UPDATED = range(5)


def scratch_of(sh):
    nz, ny, br = sh.nz, sh.ny, sh.brows
    ar, wr = sh.arows, sh.wrows
    operands = [
        (5, 2, D),
        (ar, 3 * D),
        (ar, D),
        (2, ar),
        (2, ar),
        (ar, 2, MEM),
        (wr, D),
        (wr, D),
        (br, TP * 2 * sh.pc),
        (48, SMALL),
        (4, MEM, SMALL),
        (sh.xrows, ny * 2 * sh.pc),
    ]
    jobs = {(STAGED, i, 0): (dims, BF16) for i, dims in enumerate(operands)}
    s = dict(
        pk=((2, sh.pr, ACOLS), BF16),
        ff=((2, sh.fr, D), BF16),
        gms=((2, 8, D), F32),
        p1=((2, sh.pr, ACOLS), BF16),
        p2=((TP, 2 * sh.pc, REST), BF16),
        p2y=((ny, 2 * sh.pc, HALF), BF16),
        turn=((D, D), BF16),
        xp=((ROWS, D), BF16),
        wx=((TP, nz, sh.xrows, HALF), BF16),
        gx=((TP, nz, sh.xrows, HALF), BF16),
        f1=((2, sh.fr, D), BF16),
        wa=((nz, ny, br, ACOLS), BF16),
        wf=((TP, nz, ny, br, D), BF16),
        wo=((2, nz, ny, br, HALF), BF16),
        par=((8, D), F32),
        x=((ROWS, D), BF16),
        gyt=((TP * TOKENS, D), BF16),
        gm=((2, 8, D), F32),
        qkv=((9, ROWS, 128), BF16),
        pt=((6, ROWS, ROWS), BF16),
        ot=((3, 128, ROWS), BF16),
        oc=((ROWS, HALF), BF16),
        oin=((OWN, HALF), BF16),
        h1=((OWN, D), F32),
        n1=((OWN, D), F32),
        inv1=((OWN, 1), F32),
        h1b=((ROWS, D), BF16),
        gl=((2, ROWS, D), BF16),
        sl=((2, ROWS, D), BF16),
        fs=((OWN, D), BF16),
        fr=((OWN, D), BF16),
        n2=((OWN, D), F32),
        yb=((OWN, D), BF16),
        mo=((2, 8, D), F32),
        hop=((16, D), BF16),
        hopin=((16, D), BF16),
        es=((16, D), F32),
        er=((16, D), F32),
        dz=((OWN, D), F32),
        dfb=((ROWS, D), BF16),
        du=((2, ROWS, D), BF16),
        dhs=((OWN, D), BF16),
        dhr=((OWN, D), BF16),
        dr=((OWN, D), F32),
        dab=((ROWS, D), BF16),
        doc=((3, ROWS, 128), BF16),
        dqkv=((9, ROWS, 128), BF16),
        ga=((nz, ny, br, ACOLS), BF16),
        gi=((TP, nz, ny, br, HALF), BF16),
        gt=((TP, nz, ny, br, HALF), BF16),
        dxs=((OWN, D), BF16),
        dxr=((OWN, D), BF16),
        dxb=((TP * TOKENS, D), BF16),
        sg=((48, D), F32),
        e3=((TP, 2 * sh.pc, REST), BF16),
        r3=((TP - 1, 2 * sh.pc, REST), BF16),
        e3y=((ny, 2 * sh.pc, HALF), BF16),
        r3y=((max(1, ny - 1), 2 * sh.pc, HALF), BF16),
        s4=((2, sh.pc, ACOLS), F32),
        sf=((2, sh.wrows, D), F32),
    )
    s.update(gos=((nz // 2, ny, br, HALF) if nz > 1 else (1, 1, HALF, HALF), BF16))
    sizes = {"x": TP, "z": nz, "y": ny}
    for name, order, cols, axes in scatter_jobs():
        left = [a for a in axes]
        block = (sh.xrows if name[0] == "x" else br, cols.stop - cols.start)
        for step, axis in enumerate(order):
            left = [a for a in left if a != axis]
            dims = tuple(sizes[a] for a in left)
            ring = step == 0 and name in RINGS and sizes[axis] == 4
            jobs[LANDED, step, name] = ((2 if ring else max(1, sizes[axis] - 1),) + dims + block, BF16)
            if step < len(order) - 1:
                jobs[SUMMED, step, name] = (dims + block, BF16)
            if ring:
                jobs[PASSED, 0, name] = ((2, dims[0] // 2) + dims[1:] + block, BF16)
                jobs[UPDATED, 0, name] = jobs[PASSED, 0, name]
    return s, jobs


def scatter_jobs():
    orders = [("z", "y", "x"), ("x", "z", "y"), ("y", "x", "z")]
    jobs = []
    for kind in ("t", "i"):
        for j in range(3):
            jobs.append((f"{kind}{j}", orders[j], slice(128 * j, 128 * j + 128), ("x", "z", "y")))
    zy, yz = ("z", "y"), ("y", "z")
    jobs.append(("aw", yz, slice(WO, WO + HALF), zy))
    jobs.append(("x0", ("x", "z"), slice(0, HALF), ("x", "z")))
    jobs.append(("a1", zy, slice(HALF, 2 * HALF), zy))
    jobs.append(("a2", yz, slice(2 * HALF, 2 * HALF + 256), zy))
    jobs.append(("a3", zy, slice(2 * HALF + 256, 3 * HALF), zy))
    jobs.append(("as", zy, slice(4 * HALF, ACOLS), zy))
    return jobs


def gather_jobs():
    orders = [("x", "y", "z"), ("y", "z", "x"), ("z", "x", "y")]
    jobs = [(f"f{j}", orders[j], slice(256 * j, 256 * j + 256), ("x", "z", "y")) for j in range(3)]
    jobs.append(("x0", ("z", "x"), slice(0, HALF), ("x", "z")))
    jobs.append(("a0", ("y", "z"), slice(HALF, CUT), ("z", "y")))
    jobs.append(("a1", ("z", "y"), slice(CUT, ACOLS), ("z", "y")))
    return jobs


RINGS = ("t0", "t1", "t2", "i0", "i1", "i2", "aw", "x0", "a1")
WEIGHTS = {"f": "wf", "a": "wa", "x": "wx"}
GRADS = {"t": "gt", "i": "gi", "a": "ga", "x": "gx"}


def kernel(sh, names, *refs):
    xin, gin = refs[:2]
    hout, mout, dxo, gao, gfo = refs[15:20]
    ssem, rsem, xsem, lsem = refs[-4:]
    count = len(names[0])
    b = types.SimpleNamespace(**dict(zip(names[0], refs[20 : 20 + count])))
    k = dict(zip(names[1], refs[20 + count : -4]))
    staged = [k[STAGED, i, 0] for i in range(12)]
    gmem, wq, wp, gain_in, bias_in, token_in, up_in, down_in = staged[:8]
    packsel, smallsel, places, packy = staged[8:]
    turn = refs[14]
    nz, ny, br, wr, ar = sh.nz, sh.ny, sh.brows, sh.wrows, sh.arows
    pk, ff, gms = b.pk, b.ff, b.gms

    dp = lax.axis_index("dp")
    x = lax.axis_index("tp")
    core = dp % 2
    y = (dp // 2) % ny
    z = dp // (2 * ny)
    other = 1 - core
    chain = x // 2
    seg = jnp.where((x == 1) | (x == 2), 1, 0)
    at = {"x": x, "y": y, "z": z}
    size = {"x": TP, "y": ny, "z": nz}

    def device(x_=x, y_=y, z_=z, c_=core):
        return ((z_ * ny + y_) * 2 + c_, x_)

    near = {a: [(at[a] + o) % size[a] for o in range(size[a])] for a in at}

    def moved_to(axis, offset, core_=core):
        there = dict(at)
        there[axis] = near[axis][offset]
        return device(there["x"], there["y"], there["z"], core_)

    neighbours = {a: [moved_to(a, o) for o in range(size[a])] for a in at}

    def moved(axis, offset):
        return neighbours[axis][offset]

    sibling = device(c_=other)
    sent = []

    class Group:
        def __init__(self, like):
            if len(sent) >= SENDS:
                sent[-SENDS].wait_send()
            self.like = like
            self.number = len(sent)
            sent.append(self)

        def add(self, src, dst, to):
            pltpu.make_async_remote_copy(
                src_ref=src,
                dst_ref=dst,
                send_sem=ssem.at[self.number % SENDS],
                recv_sem=rsem.at[self.number],
                device_id=to,
                device_id_type=MESH,
            ).start()

        def wait_send(self):
            like = self.like()
            pltpu.make_async_copy(like, like, ssem.at[self.number % SENDS]).wait()

        def wait_recv(self):
            like = self.like()
            pltpu.make_async_copy(like, like, rsem.at[self.number]).wait()

    def remote(src, dst, to):
        where = dst if callable(dst) else lambda: dst
        group = Group(where)
        group.add(src, where(), to)
        return group

    def arrived(groups):
        for group in groups:
            group.wait_recv()

    locals_ = [0]

    def local(src, dst):
        copy = pltpu.make_async_copy(src, dst, lsem.at[locals_[0]])
        locals_[0] += 1
        copy.start()
        return copy

    staging = [local(refs[2 + i], staged[i]) for i in range(12)]
    turn_local = local(turn, b.turn)

    barrier = pltpu.get_barrier_semaphore()
    peers = [sibling]
    for o in range(1, TP):
        peers += [moved("x", o), moved_to("x", o, other)]
    for axis in ("y", "z"):
        for o in range(1, size[axis]):
            peers.append(moved(axis, o))
    for peer in peers:
        pl.semaphore_signal(barrier, inc=1, device_id=peer, device_id_type=MESH)

    pk[...] = jnp.zeros(pk.shape, BF16)
    ff[...] = jnp.zeros(ff.shape, BF16)
    gms[...] = jnp.zeros(gms.shape, F32)
    for copy in staging:
        copy.wait()
    small = dot(gain_in[...], places[0, :2], TN) + dot(bias_in[...], places[1, :2], TN)
    small = small + dot(token_in[:, 0], places[2]) + dot(token_in[:, 1], places[3])
    small = small.astype(BF16)
    for h in range(2):
        for p in range(3):
            for i in range(3):
                first = D * i + HALF * h + 128 * p
                pk[h, :ar, HALF * p + 128 * i : HALF * p + 128 * (i + 1)] = wq[:, first : first + 128]
        pk[h, :ar, WO : WO + HALF] = wp[:, HALF * h : HALF * (h + 1)]
        pk[h, :ar, 4 * HALF :] = small
        for j in range(3):
            cols = slice(HALF * h + 128 * j, HALF * h + 128 * (j + 1))
            ff[h, :wr, 256 * j : 256 * j + 128] = up_in[:, cols]
            ff[h, :wr, 256 * j + 128 : 256 * j + 256] = down_in[:, cols]
        gms[h, 0:5] = gmem[:, h].astype(F32)
    pl.semaphore_wait(barrier, len(peers))

    pk_local = local(pk.at[core], b.p1.at[core])
    ff_local = local(ff.at[core], b.f1.at[core])
    pk_swap = remote(pk.at[other], b.p1.at[core], sibling)
    ff_swap = remote(ff.at[other], b.f1.at[core], sibling)

    conditional = []

    def to_device(src, dst, place, here, kind, send_slot):
        copy = pltpu.make_async_remote_copy(
            src_ref=src,
            dst_ref=dst,
            send_sem=xsem.at[25 + XBASE[kind] + send_slot],
            recv_sem=here,
            device_id=device(x_=place[0], c_=place[1]),
            device_id_type=MESH,
        )
        same = (place[0] == x) & (place[1] == core)

        @pl.when(same)
        def _():
            pltpu.make_async_copy(src, dst, here).start()

        @pl.when(jnp.logical_not(same))
        def _():
            copy.start()

        conditional.append((same, copy))

    def from_device(dst, kind, slot):
        pltpu.make_async_copy(dst, dst, xsem.at[XBASE[kind] + slot]).wait()

    def chip_of(k, s):
        return s + k * (3 - 2 * s)

    def send_rows():
        for s in range(2):
            for j in range(2):
                to_device(
                    xin.at[s, pl.ds(TOKENS * j, TOKENS)],
                    b.x.at[pl.ds(pl.multiple_of(OWN * j + TOKENS * x, 16), TOKENS)],
                    (chip_of(core, s), j),
                    xsem.at[XBASE[0] + x],
                    0,
                    2 * s + j,
                )

    def send_upstream():
        for s in range(2):
            for j in range(2):
                to_device(
                    gin.at[s, pl.ds(TOKENS * j, TOKENS)],
                    b.gyt.at[pl.ds(pl.multiple_of(TOKENS * x, 16), TOKENS)],
                    (chip_of(core, s), j),
                    xsem.at[XBASE[1] + x],
                    1,
                    2 * s + j,
                )
            to_device(
                gms.at[s], b.gm.at[x % 2], (chip_of(core, s), x // 2), xsem.at[XBASE[2] + x % 2], 2, s
            )

    def part_of(job, step, place, half=None):
        name, order, cols, axes = job
        fixed = {a: at[a] for a in order[step:]}
        fixed[order[step]] = place
        where = []
        for a in axes:
            if a in fixed:
                where.append(fixed[a])
            elif half is not None:
                where.append(pl.ds(half * (size[a] // 2), size[a] // 2))
                half = None
            else:
                where.append(slice(None))
        return getattr(b, WEIGHTS[name[0]]).at[tuple(where) + (slice(None), cols)]

    def gather_start(name, step):
        job = gathers[name]
        axis = job[1][step]
        n = size[axis]
        own = part_of(job, step, at[axis])
        free = [a for a in job[3] if a not in job[1][step:]]
        relay = n == 4 and step == len(job[1]) - 1 and size[free[0]] % 2 == 0
        state = types.SimpleNamespace(step=step, relay=relay)
        if relay:
            first = [part_of(job, step, at[axis], h) for h in range(2)]
            right, left = moved(axis, 1), moved(axis, n - 1)
            state.right, state.left = (
                remote(first[h], lambda h=h: part_of(job, step, at[axis], h), to) for h, to in ((0, right), (1, left))
            )
            state.every = [Group(lambda: part_of(job, step, pl.ds(0, 2)))]
            state.every[0].add(first[1], first[1], right)
            state.every[0].add(first[0], first[0], left)
        else:
            state.every = [Group(lambda: part_of(job, step, pl.ds(0, n - 1)))] if n > 1 else []
            for o in range(1, n):
                state.every[0].add(own, own, moved(axis, o))
        flying[name] = state

    def gather_pass(name):
        job, state = gathers[name], flying[name]
        if not state.relay:
            return
        axis = job[1][state.step]
        n = size[axis]
        for copy, back, onward, half in ((state.right, n - 1, 1, 0), (state.left, 1, n - 1, 1)):
            arrived([copy])
            piece = part_of(job, state.step, near[axis][back], half)
            state.every[0].add(piece, piece, moved(axis, onward))

    def gather_done(name):
        arrived(flying[name].every)

    gathers = {j[0]: j for j in gather_jobs()}
    flying = {}

    pk_local.wait()
    arrived([pk_swap])
    packed = jnp.concatenate([b.p1[c].astype(F32)[: sh.pc] for c in range(2)], 0).astype(BF16)
    b.p2y[y] = packed[:, :HALF]
    b.p2[x] = packed[:, HALF:]
    mine = b.p2y.at[y]
    ysteps, xsteps = [], [Group(lambda: b.p2.at[: TP - 1])]
    if ny > 1:
        ysteps.append(Group(lambda: b.p2y.at[: ny - 1]))
    for o in range(1, ny):
        ysteps[0].add(mine, mine, moved("y", o))
    mine = b.p2.at[x]
    for o in range(1, TP):
        xsteps[0].add(mine, mine, moved("x", o))
    ff_local.wait()
    arrived([ff_swap])
    two = [b.f1[c].astype(F32)[:wr] for c in range(2)]
    b.wf[x, z, y] = jnp.concatenate(two, 0).astype(BF16)
    feed_names, first_names = ("f1", "f2", "f0"), ("x0", "a0", "a1")
    for n in feed_names:
        gather_start(n, 0)
    send_rows()
    arrived(ysteps)
    b.wx[x, z] = dot(packy[...], b.p2y[...].reshape(ny * 2 * sh.pc, HALF)).astype(BF16)
    gather_start("x0", 0)
    arrived(xsteps)
    b.wa[z, y, :, HALF:] = dot(packsel[...], b.p2[...].reshape(TP * 2 * sh.pc, REST)).astype(BF16)
    for n in ("a0", "a1"):
        gather_start(n, 0)
    for n in feed_names:
        gather_done(n)
        gather_start(n, 1)
    for n in first_names:
        gather_done(n)
        gather_start(n, 1)
    for n in first_names:
        gather_pass(n)
    for n in feed_names:
        gather_done(n)
        gather_start(n, 2)

    for i in range(TP):
        from_device(b.x.at[pl.ds(pl.multiple_of(OWN * core + TOKENS * i, 16), TOKENS)], 0, i)
    half = b.x.at[pl.ds(pl.multiple_of(OWN * core, 16), TP * TOKENS)]
    x_swap = remote(half, half, sibling)
    for first in (256, OWN + 256):
        b.x[first : first + 16] = jnp.zeros((16, D), BF16)
    turn_local.wait()
    arrived([x_swap])

    @pl.loop(0, 2)
    def _(i):
        rows = pl.ds(pl.multiple_of(OWN * i, 16), OWN)
        b.xp[rows] = dot(b.x[rows], b.turn[...], NT).astype(BF16)

    for n in first_names:
        gather_done(n)
    wo_cols = slice(WO, WO + HALF)
    wo_local = local(b.wa.at[:, :, :, wo_cols], b.wo.at[core])
    wo_swap = remote(b.wa.at[:, :, :, wo_cols], b.wo.at[core], sibling)
    gather_pass("f1")
    send_upstream()

    def attention_weight():
        return b.wa[:, :, :, :WO].reshape(D, WO)

    small = b.wa[:, :, :, 4 * HALF :].reshape(D, SMALL)
    chosen = dot(smallsel[...], small, NT)
    b.par[...] = chosen[0:8]
    memory = chosen[16:48].astype(BF16)
    b.x[OWN + 256 : OWN + 272] = memory[16:]
    turned = dot(memory, b.turn[...], NT).astype(BF16)
    b.xp[OWN + 256 : OWN + 272] = turned[16:]

    @pl.when(seg == 0)
    def _():
        b.x[256:272] = memory[:16]
        b.xp[256:272] = turned[:16]

    gains = [b.par[i : i + 1] for i in range(2)]
    biases = [b.par[2 + i : 3 + i] for i in range(2)]

    hop_to = jnp.where(x == 0, 1, 2)
    hops = []
    for j in range(2):
        hops.append(
            pltpu.make_async_remote_copy(
                src_ref=b.hop,
                dst_ref=b.hopin,
                send_sem=xsem.at[XBASE[6] + j],
                recv_sem=xsem.at[XBASE[6] + 2],
                device_id=device(x_=hop_to, c_=j),
                device_id_type=MESH,
            )
        )

    own_rows = pl.ds(pl.multiple_of(OWN * core, 16), OWN)
    other_rows = pl.ds(pl.multiple_of(OWN * other, 16), OWN)

    out = dot(b.xp[...], b.wx[...].reshape(D, HALF)).astype(BF16)
    for i in range(3):
        b.qkv[i] = out[:, 128 * i : 128 * i + 128]
    out = dot(b.x[...], b.wa[:, :, :, HALF:WO].reshape(D, 2 * HALF)).astype(BF16)
    for i in range(3, 9):
        b.qkv[i] = out[:, 128 * (i - 3) : 128 * (i - 2)]

    def head_masks(hh):
        lane = lax.broadcasted_iota(jnp.int32, (ROWS, 128), 1)
        row = lax.broadcasted_iota(jnp.int32, (ROWS, 128), 0)
        inside = (lane // 64) == hh
        spare = lane == 64 * (1 - hh)
        memory = ((row >= 256) & (row < 272)) | (row >= OWN + 256)
        invalid = memory & (row % 8 >= 5)
        return inside, spare, invalid

    def forward_pair(p):
        qp, kp, vp = (b.qkv[3 * p + i] for i in range(3))
        vt = vp.T
        for hh in range(2):
            inside, spare, invalid = head_masks(hh)
            zero = jnp.zeros_like(kp)
            kmask = jnp.where(spare & invalid, jnp.full_like(kp, MASKED), zero)
            km = jnp.where(inside, kp, kmask)
            qm = jnp.where(inside, qp, jnp.where(spare, jnp.ones_like(qp), zero))
            scores = dot(km, qm, NT)
            peak = jnp.max(scores, 0, keepdims=True)
            raised = jnp.exp2((scores - peak) * EXP_SCALE)
            total = jnp.sum(raised, 0, keepdims=True)
            probs = (raised * (1.0 / total)).astype(BF16)
            b.pt[2 * p + hh] = probs
            b.ot[p, 64 * hh : 64 * hh + 64] = dot(vt[64 * hh : 64 * hh + 64], probs).astype(BF16)
        b.oc[:, pl.ds(pl.multiple_of(128 * p, 128), 128)] = b.ot[p].T

    @pl.loop(0, 3)
    def _(j):
        cols = pl.ds(pl.multiple_of(128 * j, 128), 128)
        block = dot(b.turn[...], b.wx[:, :, :, cols].reshape(D, 128), TN).astype(BF16)
        b.wa[:, :, :, cols] = block.reshape(nz, ny, br, 128)

    @pl.loop(0, 6)
    def _(i):
        @pl.when((i // 3) == seg)
        def _():
            forward_pair(i % 3)

        @pl.when(i == 1)
        def _():
            for n in ("f2", "f0"):
                gather_pass(n)

        @pl.when((i == 2) & (seg == 1))
        def _():
            hops[0].wait_recv()
            b.x[256:272] = b.hopin[...]
            b.xp[256:272] = dot(b.hopin[...], b.turn[...], NT).astype(BF16)
            rows = dot(b.hopin[...], attention_weight()).astype(BF16)
            for j in range(9):
                b.qkv[j, 256:272] = rows[:, 128 * j : 128 * j + 128]

    def head_rows(ref, c):
        if nz > 1:
            return ref.at[pl.ds(c * (nz // 2), nz // 2)]
        return ref.at[:, :, pl.ds(pl.multiple_of(c * HALF, 16), HALF)]

    def wo_rows(h, c):
        return head_rows(b.wo.at[h], c)[...].reshape(HALF, HALF)

    o_swap = remote(b.oc.at[other_rows], b.oin, sibling)
    wo_local.wait()
    arrived([wo_swap])
    halves = [dot(b.oc[own_rows], wo_rows(h, core)) for h in range(2)]
    arrived([o_swap])
    attended = jnp.concatenate([halves[h] + dot(b.oin[...], wo_rows(h, other)) for h in range(2)], 1)
    h1, n1, inv1 = norm_forward(b.x[own_rows].astype(F32) + attended, gains[0], biases[0])
    b.h1[...] = h1
    b.n1[...] = n1
    b.inv1[...] = inv1
    b.h1b[own_rows] = h1.astype(BF16)
    h_swap = remote(b.h1b.at[own_rows], b.h1b.at[own_rows], sibling)
    for n in ("f1", "f2", "f0"):
        gather_done(n)

    def feed_weight(t, kind):
        cols = [256 * j + 128 * kind for j in range(3)]
        blocks = [b.wf[2 * t + i, :, :, :, c : c + 128].reshape(D, 128) for i in range(2) for c in cols]
        return jnp.concatenate(blocks, 1)

    def up_weight(t):
        return feed_weight(t, 0)

    def down_weight(t):
        return feed_weight(t, 1)

    def activate(units):
        erf = 0.5 * (1.0 + lax.erf(units * INV_ROOT_TWO))
        return (units * erf).astype(BF16), erf

    early = pltpu.make_async_remote_copy(
        src_ref=b.es,
        dst_ref=b.er,
        send_sem=xsem.at[XBASE[6] + 3],
        recv_sem=xsem.at[XBASE[6] + 4],
        device_id=sibling,
        device_id_type=MESH,
    )
    row16 = lax.broadcasted_iota(jnp.int32, (16, D), 0)

    @pl.when(seg == 0)
    def _():
        arrived([h_swap])
        rows = b.h1b[OWN + 256 : OWN + 272]
        part = sum(dot(activate(dot(rows, up_weight(t)))[0], down_weight(t), NT) for t in range(2))

        @pl.when(core == 0)
        def _():
            b.es[...] = part
            early.start()

        @pl.when(core == 1)
        def _():
            early.wait_recv()
            whole = b.h1[256:272] + part + b.er[...]
            written = norm_forward(whole, gains[1], biases[1])[0]
            b.hop[...] = jnp.where(row16 % 8 < 5, written, 0.0).astype(BF16)
            hops[0].start()
            hops[1].start()

    def project_up(rows):
        for t in range(2):
            units = dot(b.h1b[rows], up_weight(t))
            active, erf = activate(units)
            b.gl[t, rows] = active
            b.sl[t, rows] = (erf + units * jnp.exp(-0.5 * units * units) * INV_ROOT_TWOPI).astype(BF16)

    @pl.loop(0, 2)
    def _(i):
        @pl.when((i == 1) & (seg == 1))
        def _():
            arrived([h_swap])

        project_up(pl.ds(pl.multiple_of(OWN * jnp.where(i == 0, core, other), 16), OWN))


    def partial_down(rows):
        return sum(dot(b.gl[t, rows], down_weight(t), NT) for t in range(2))

    b.fs[...] = partial_down(other_rows).astype(BF16)
    f_swap = remote(b.fs, b.fr, sibling)
    branch = partial_down(own_rows)
    arrived([f_swap])
    out, n2, inv2 = norm_forward(b.h1[...] + branch + b.fr[...].astype(F32), gains[1], biases[1])
    low = out.astype(BF16)
    b.yb[...] = low
    b.mo[...] = low[256:272].astype(F32).reshape(2, 8, D)
    for i in range(TP):
        to_device(
            b.yb.at[pl.ds(TOKENS * i, TOKENS)],
            hout.at[seg, pl.ds(pl.multiple_of(TOKENS * core, 16), TOKENS)],
            (i, chain),
            xsem.at[XBASE[3] + 2 * seg + core],
            3,
            i,
        )
    for i in range(2):
        to_device(b.mo.at[i], mout.at[seg], (2 * core + i, chain), xsem.at[XBASE[4] + seg], 4, i)

    for i in range(TP):
        from_device(b.gyt.at[pl.ds(TOKENS * i, TOKENS)], 1, i)
    for i in range(2):
        from_device(b.gm.at[i], 2, i)
    upstream = jnp.concatenate([b.gyt[...].astype(F32), b.gm[...].reshape(16, D)], 0)
    b.sg[...] = jnp.zeros((48, D), F32)
    b.sg[1:2] = column_sum(upstream * n2)
    b.sg[3:4] = column_sum(upstream)
    dz = norm_backward(upstream, n2, inv2, gains[1])
    b.dz[...] = dz
    b.dfb[own_rows] = dz.astype(BF16)
    df_swap = remote(b.dfb.at[own_rows], b.dfb.at[own_rows], sibling)

    def weight_grad(into, left, right):
        @pl.loop(0, 2)
        def _(t):
            part = dot(left[...], right[t], TN).astype(BF16)
            for i in range(2):
                into[2 * t + i] = part[:, HALF * i : HALF * (i + 1)].reshape(nz, ny, br, HALF)

    scatters = {j[0]: j for j in scatter_jobs()}
    rs = {}

    def is_ring(name, step):
        _, order, cols, axes = scatters[name]
        return step == 0 and name in RINGS and size[order[0]] == 4

    def source_of(name, step):
        _, order, cols, axes = scatters[name]
        axis = order[step]
        left = [a for a in axes if a not in order[:step]]
        array = getattr(b, GRADS[name[0]]) if step == 0 else k[SUMMED, step - 1, name]
        tail = (slice(None), cols) if step == 0 else ()

        def part(place, half=None):
            where = []
            for a in left:
                if a == axis:
                    where.append(place)
                elif half is not None:
                    where.append(pl.ds(half * (size[a] // 2), size[a] // 2))
                    half = None
                else:
                    where.append(slice(None))
            return array.at[tuple(where) + tail]

        return part

    def scatter_send(name, step):
        axis = scatters[name][1][step]
        n = size[axis]
        part = source_of(name, step)
        landing = k[LANDED, step, name]
        if is_ring(name, step):
            right, left, far = (near[axis][o] for o in (1, n - 1, 2))
            to_right, to_left = moved(axis, 1), moved(axis, n - 1)
            half = size[[a for a in scatters[name][3] if a != axis][0]] // 2
            over = k[PASSED, 0, name]
            passing = [
                remote(part(far, 0), lambda: over.at[0], to_right),
                remote(part(far, 1), lambda: over.at[1], to_left),
            ]
            coming = Group(lambda: landing)
            coming.add(part(right, 1), landing.at[0, half:], to_right)
            coming.add(part(left, 0), landing.at[1, :half], to_left)
            rs[name] = (passing, coming, half, (right, left), (to_right, to_left))
            return
        rs[name] = [Group(lambda: landing)] if n > 1 else []
        for o in range(1, n):
            rs[name][0].add(part(near[axis][o]), landing.at[o - 1], moved(axis, o))

    def scatter_pass(name):
        if not is_ring(name, 0):
            return
        passing, coming, half, places_, devices = rs[name]
        part = source_of(name, 0)
        landing, over, updated = k[LANDED, 0, name], k[PASSED, 0, name], k[UPDATED, 0, name]
        for i in range(2):
            arrived([passing[i]])
            updated[i] = (part(places_[i], i)[...].astype(F32) + over[i].astype(F32)).astype(BF16)
            where = landing.at[0, :half] if i == 0 else landing.at[1, half:]
            coming.add(updated.at[i], where, devices[i])

    def scatter_sum(name, step):
        _, order, cols, axes = scatters[name]
        axis = order[step]
        total = source_of(name, step)(at[axis])[...].astype(F32)
        ring = is_ring(name, step)
        arrived([rs[name][1]] if ring else rs[name])
        for o in range(2 if ring else size[axis] - 1):
            total = total + k[LANDED, step, name][o].astype(F32)
        if step < len(order) - 1:
            k[SUMMED, step, name][...] = total.astype(BF16)
        return total

    def scatter_on(names, step):
        for n in names:
            scatter_sum(n, step)
            scatter_send(n, step + 1)

    down_names, up_names = ("t0", "t1", "t2"), ("i0", "i1", "i2")
    def units_back(rows):
        for t in range(2):
            b.du[t, rows] = (dot(b.dfb[rows], down_weight(t)) * b.sl[t, rows].astype(F32)).astype(BF16)

    units_back(own_rows)
    arrived([df_swap])
    weight_grad(b.gt, b.dfb, b.gl)
    for n in down_names:
        scatter_send(n, 0)
    units_back(other_rows)

    def partial_up(rows):
        return sum(dot(b.du[t, rows], up_weight(t), NT) for t in range(2))

    b.dhs[...] = partial_up(other_rows).astype(BF16)
    dh_swap = remote(b.dhs, b.dhr, sibling)
    b.dz[...] = b.dz[...] + partial_up(own_rows)
    weight_grad(b.gi, b.h1b, b.du)
    for n in up_names:
        scatter_send(n, 0)
    for n in down_names:
        scatter_pass(n)
    arrived([dh_swap])
    into_first = b.dz[...] + b.dhr[...].astype(F32)
    b.sg[0:1] = column_sum(into_first * b.n1[...])
    b.sg[2:3] = column_sum(into_first)
    dr = norm_backward(into_first, b.n1[...], b.inv1[...], gains[0])
    b.dr[...] = dr
    b.dab[own_rows] = dr.astype(BF16)
    da_swap = remote(b.dab.at[own_rows], b.dab.at[own_rows], sibling)

    def grad_mixed(rows):
        parts = [dot(b.dab[rows, HALF * h : HALF * (h + 1)], wo_rows(h, core), NT) for h in range(2)]
        for p in range(3):
            b.doc[p, rows] = (parts[0] + parts[1])[:, 128 * p : 128 * p + 128].astype(BF16)

    grad_mixed(own_rows)
    arrived([da_swap])
    grad_mixed(other_rows)

    mixed_t = b.ot[...].reshape(HALF, ROWS)

    def proj_grad(h):
        cols = pl.ds(pl.multiple_of(HALF * h, 128), HALF)
        return dot(mixed_t, b.dab[:, cols]).astype(BF16).reshape(b.gos.shape)

    def wo_part(c):
        return head_rows(b.ga.at[:, :, :, wo_cols], c)

    b.gos[...] = proj_grad(other)
    go_swap = remote(b.gos, wo_part(core), sibling)
    wo_part(core)[...] = proj_grad(core)

    def backward_pair(p):
        qp, kp, vp = (b.qkv[3 * p + i] for i in range(3))
        dop = b.doc[p]
        kt = kp.T
        dv = dk = 0.0
        dq = []
        for hh in range(2):
            inside, _, _ = head_masks(hh)
            zero = jnp.zeros_like(kp)
            grad_probs = dot(jnp.where(inside, vp, zero), dop, NT)
            low_probs = b.pt[2 * p + hh]
            probs = low_probs.astype(F32)
            row_term = jnp.sum(probs * grad_probs, 0, keepdims=True)
            ds = (probs * (grad_probs - row_term)).astype(BF16)
            dv = dv + dot(low_probs, jnp.where(inside, dop, zero))
            dk = dk + dot(ds, jnp.where(inside, qp, zero))
            dq.append(dot(kt[64 * hh : 64 * hh + 64], ds))
        b.dqkv[3 * p] = (jnp.concatenate(dq, 0) * 0.125).T.astype(BF16)
        b.dqkv[3 * p + 1] = (dk * 0.125).astype(BF16)
        b.dqkv[3 * p + 2] = dv.astype(BF16)

    def joined(rows, wanted):
        return jnp.concatenate([b.dqkv[i, rows] for i in wanted], 1)

    def attention_grad(p):
        grads = jnp.concatenate([b.dqkv[3 * p + i] for i in range(3)], 1)

        @pl.when(p == 0)
        def _():
            b.gx[...] = dot(b.xp[...], grads, TN).astype(BF16).reshape(TP, nz, sh.xrows, HALF)

        @pl.when(p > 0)
        def _():
            cols = pl.ds(pl.multiple_of(HALF * p, 128), HALF)
            b.ga[:, :, :, cols] = dot(b.x[...], grads, TN).astype(BF16).reshape(nz, ny, br, HALF)

    @pl.loop(0, 3)
    def _(p):
        backward_pair(p)
        attention_grad(p)

        @pl.when(p == 0)
        def _():
            arrived([go_swap])
            scatter_send("aw", 0)
            scatter_send("x0", 0)

        @pl.when(p == 1)
        def _():
            for n in up_names:
                scatter_pass(n)
            scatter_send("a1", 0)
            scatter_on(down_names, 0)
            for n in ("aw", "x0"):
                scatter_pass(n)

        @pl.when(p == 2)
        def _():
            scatter_send("a2", 0)
            scatter_send("a3", 0)
            scatter_pass("a1")


    def partial_input(rows):
        return dot(joined(rows, range(9)), attention_weight(), NT)

    b.dxs[...] = partial_input(other_rows).astype(BF16)
    dx_swap = remote(b.dxs, b.dxr, sibling)
    dx = partial_input(own_rows) + b.dr[...]
    arrived([dx_swap])
    dx = dx + b.dxr[...].astype(F32)
    b.dxb[...] = dx[:256].astype(BF16)
    for i in range(TP):
        to_device(
            b.dxb.at[pl.ds(TOKENS * i, TOKENS)],
            dxo.at[seg, pl.ds(pl.multiple_of(TOKENS * core, 16), TOKENS)],
            (i, chain),
            xsem.at[XBASE[5] + 2 * seg + core],
            5,
            i,
        )

    @pl.when((core == 0) & (seg == 0))
    def _():
        b.sg[16:32] = dx[256:272]

    @pl.when(core == 1)
    def _():
        b.sg[32:48] = dx[256:272]

    small_grads = dot(b.sg[...].astype(BF16), smallsel[...], TN).astype(BF16)
    b.ga[:, :, :, 4 * HALF :] = small_grads.reshape(nz, ny, br, SMALL)
    scatter_send("as", 0)
    attention_names = ("aw", "x0", "a1", "a2", "a3", "as")
    scatter_on(up_names, 0)
    scatter_on(down_names, 1)
    scatter_on(attention_names, 0)
    scatter_on(up_names, 1)

    def last_rows(names, first_col):
        for j, n in enumerate(names):
            total = scatter_sum(n, 2)
            cols = slice(first_col + 128 * j, first_col + 128 * j + 128)
            b.sf[0, :, cols] = total[:wr]
            b.sf[1, :, cols] = total[wr:]

    for n in attention_names:
        cols = scatters[n][2]
        total = scatter_sum(n, 1).astype(BF16)
        if n == "x0":
            spread = dot(packy[...], total, TN).astype(BF16)
            b.e3y[...] = spread.reshape(ny, 2 * sh.pc, HALF)
            ysteps = [Group(lambda: b.r3y)] if ny > 1 else []
            for o in range(1, ny):
                ysteps[0].add(b.e3y.at[(y + o) % ny], b.r3y.at[o - 1], moved("y", o))
        else:
            spread = dot(packsel[...], total, TN).astype(BF16)
            b.e3[:, :, cols.start - HALF : cols.stop - HALF] = spread.reshape(TP, 2 * sh.pc, cols.stop - cols.start)
    steps = [Group(lambda: b.r3)]
    for o in range(1, TP):
        steps[0].add(b.e3.at[(x + o) % TP], b.r3.at[o - 1], moved("x", o))
    last_rows(down_names, HALF)
    last_rows(up_names, 0)
    sf_local = local(b.sf.at[core], gfo.at[core])
    sf_swap = remote(b.sf.at[other], gfo.at[core], sibling)

    arrived(steps)
    total = b.e3[x].astype(F32)
    for o in range(1, TP):
        total = total + b.r3[o - 1].astype(F32)
    b.s4[:, :, HALF:] = total.reshape(2, sh.pc, REST)
    arrived(ysteps)
    total = b.e3y[y].astype(F32)
    for o in range(1, ny):
        total = total + b.r3y[o - 1].astype(F32)
    b.s4[:, :, :HALF] = total.reshape(2, sh.pc, HALF)
    s4_local = local(b.s4.at[core], gao.at[core])
    s4_swap = remote(b.s4.at[other], gao.at[core], sibling)

    for kind, out_ref in ((3, hout), (5, dxo)):
        for s in range(2):
            for j in range(2):
                from_device(out_ref.at[s, pl.ds(TOKENS * j, TOKENS)], kind, 2 * s + j)
    for s in range(2):
        from_device(mout.at[s], 4, s)
    sf_local.wait()
    s4_local.wait()
    arrived([sf_swap, s4_swap])

    for group in sent[-SENDS:]:
        group.wait_send()
    for same, copy in conditional:

        @pl.when(jnp.logical_not(same))
        def _():
            copy.wait_send()

    @pl.when((seg == 0) & (core == 1))
    def _():
        hops[0].wait_send()
        hops[1].wait_send()

    @pl.when((seg == 0) & (core == 0))
    def _():
        early.wait_send()


def layer(sh, arrays):
    constants = [jnp.asarray(a, BF16) for a in selections(sh)]
    tables = scratch_of(sh)
    names = [list(table) for table in tables]
    anywhere = pl.BlockSpec(memory_space=pl.ANY)
    outs = [
        jax.ShapeDtypeStruct((2, 128, D), BF16),
        jax.ShapeDtypeStruct((2, 8, D), F32),
        jax.ShapeDtypeStruct((2, 128, D), BF16),
        jax.ShapeDtypeStruct((2, sh.pc, ACOLS), F32),
        jax.ShapeDtypeStruct((2, sh.wrows, D), F32),
    ]
    return pl.pallas_call(
        functools.partial(kernel, sh, names),
        name="layer",
        out_shape=outs,
        in_specs=[anywhere] * 15,
        out_specs=[anywhere] * len(outs),
        scratch_shapes=[pltpu.VMEM(*one) for table in tables for one in table.values()]
        + [
            pltpu.SemaphoreType.DMA((SENDS,)),
            pltpu.SemaphoreType.DMA((96,)),
            pltpu.SemaphoreType.DMA((45,)),
            pltpu.SemaphoreType.DMA((20,)),
        ],
        compiler_params=pltpu.CompilerParams(
            collective_id=0, has_side_effects=True, vmem_limit_bytes=64 * 2**20 - 2**17
        ),
    )(*arrays, *constants)


def unpack_kernel(sh, *refs):
    arrays, results, held, outs, sems = refs[:5], refs[5:15], refs[15:20], refs[20:30], refs[30]
    loads = [pltpu.make_async_copy(arrays[i], held[i], sems.at[i]) for i in range(5)]
    stores = [pltpu.make_async_copy(outs[i], results[i], sems.at[5 + i]) for i in range(10)]
    for copy in loads:
        copy.start()
    hout, mout, dxo, gao, gfo = held
    hidden, memory, grad_in, gq, gp, gains, biases, tokens, gi, gt = outs
    ar = sh.arows
    loads[0].wait()
    hidden[...] = hout[...]
    stores[0].start()
    loads[2].wait()
    grad_in[...] = dxo[...].astype(F32)
    stores[2].start()
    loads[1].wait()
    for i in range(2):
        memory[:, i] = mout[i, :5].astype(BF16)
    stores[1].start()
    loads[3].wait()
    for h in range(2):
        for p in range(3):
            for i in range(3):
                to = D * i + HALF * h + 128 * p
                first = HALF * p + 128 * i
                gq[:, to : to + 128] = gao[h, :ar, first : first + 128]
        gp[:, HALF * h : HALF * (h + 1)] = gao[h, :ar, WO : WO + HALF]
    small = gao[0, :, 4 * HALF :] + gao[1, :, 4 * HALF :]
    turned = small.T[:, :ar]
    gains[...] = turned[0:2]
    biases[...] = turned[2:4]
    for kind in range(2):
        tokens[:, kind] = small[:ar, 4 + MEM * kind : 4 + MEM * (kind + 1)]
    for i in range(3, 8):
        stores[i].start()
    loads[4].wait()
    for h in range(2):
        gi[:, HALF * h : HALF * (h + 1)] = gfo[h, :, :HALF]
        gt[:, HALF * h : HALF * (h + 1)] = gfo[h, :, HALF:]
    for i in range(8, 10):
        stores[i].start()
    for copy in stores:
        copy.wait()


def unpack(sh, *arrays):
    ar, wr = sh.arows, sh.wrows
    shapes = [
        ((2, 128, D), BF16),
        ((5, 2, D), BF16),
        ((2, 128, D), F32),
        ((ar, 3 * D), F32),
        ((ar, D), F32),
        ((2, ar), F32),
        ((2, ar), F32),
        ((ar, 2, MEM), F32),
        ((wr, D), F32),
        ((wr, D), F32),
    ]
    anywhere = pl.BlockSpec(memory_space=pl.ANY)
    return pl.pallas_call(
        functools.partial(unpack_kernel, sh),
        name="unpack",
        out_shape=[jax.ShapeDtypeStruct(*one) for one in shapes],
        in_specs=[anywhere] * 5,
        out_specs=[anywhere] * len(shapes),
        scratch_shapes=[pltpu.VMEM(a.shape, a.dtype) for a in arrays]
        + [pltpu.VMEM(*one) for one in shapes]
        + [pltpu.SemaphoreType.DMA((15,))],
        compiler_params=pltpu.CompilerParams(vmem_limit_bytes=64 * 2**20 - 2**17),
    )(*arrays)


def body(
    sh,
    hidden_in,
    reset,
    w_qkv,
    w_attn_out,
    norm_gains,
    norm_biases,
    memory_tokens,
    w_in,
    w_out,
    grad_hidden,
    grad_memory,
):
    arrays = (
        hidden_in,
        grad_hidden,
        grad_memory.transpose(1, 0, 2),
        w_qkv,
        w_attn_out,
        norm_gains,
        norm_biases,
        memory_tokens.transpose(2, 0, 1),
        w_in,
        w_out.T,
    )
    hidden, memory, *middle, tokens, gi, gt = unpack(sh, *layer(sh, arrays))
    return hidden, memory.transpose(1, 0, 2), *middle, tokens.transpose(1, 2, 0), gi, gt.T


def solution(mesh):
    sh = Shape(mesh.shape["dp"])
    return jax.shard_map(
        functools.partial(body, sh),
        mesh=mesh,
        in_specs=(
            P("dp", "tp", None),
            P("dp"),
            P(("dp", "tp"), None),
            P(("dp", "tp"), None),
            P(None, ("dp", "tp")),
            P(None, ("dp", "tp")),
            P(None, None, ("dp", "tp")),
            P("dp", "tp"),
            P("tp", "dp"),
            P("dp", "tp", None),
            P("dp", "tp", None),
        ),
        out_specs=(
            P("dp", "tp", None),
            P("dp", "tp", None),
            P("dp", "tp", None),
            P(("dp", "tp"), None),
            P(("dp", "tp"), None),
            P(None, ("dp", "tp")),
            P(None, ("dp", "tp")),
            P(None, None, ("dp", "tp")),
            P("dp", "tp"),
            P("tp", "dp"),
        ),
        check_vma=False,
    )
```

profile of v0, /device:TPU:1, one launch (start us, length us, event | category | flops | bytes accessed | tf_op | source)
XLA Modules:
  0.0 118.2 jit_solution(8275809429524411451)
XLA Ops:
  0.6 115.1 %layer.1 = (bf16[2,128,768]{2,1,0:T(8,128)(2,1)}, f32[2,8,768]{2,1,0:T(8,128)}, bf16[2,128,768]{2,1,0:T(8,128)(2,1)}, f32[2,8,1664]{2,1,0:T(8,128)}, f32[2,24,768]{2,1,0:T(8,128)}) custom-call(bf16[2,128,768]{2,1,0:T(8,128)(2,1)} %refs_0_.1, bf16[2,128,768]{2,1,0:T(8,128)(2,1)} %refs_1_.1, bf16[5,2,768]{2,1,0:T(2,128)(2,1)} %bitcast.7, ...), custom_call_target="tpu_custom_call" | custom-call | tf_op jit(solution)/shard_map/layer/pallas_call | solution.py:1080
  115.8 2.3 %unpack.1 = (bf16[2,128,768]{2,1,0:T(8,128)(2,1)}, bf16[5,2,768]{2,1,0:T(2,128)(2,1)}, f32[2,128,768]{2,1,0:T(8,128)}, f32[6,2304]{1,0:T(8,128)}, f32[6,768]{1,0...) custom-call(bf16[2,128,768]{2,1,0:T(8,128)(2,1)} %get-tuple-element., ...), custom_call_target="tpu_custom_call" | custom-call | tf_op jit(solution)/shard_map/unpack/pallas_call | solution.py:1159
where the time goes:
time: 118 us
  Pallas kernels  117 us (99%)
    pallas_call x1, Pallas kernels, layer(): pl.pallas_call(functools.partial(kernel, sh, names), name='layer', out_sh...  115 us

commit v1 on v0

--- a/solution.py
+++ b/solution.py
@@ -138,7 +138,6 @@
         p2=((TP, 2 * sh.pc, REST), BF16),
         p2y=((ny, 2 * sh.pc, HALF), BF16),
         turn=((D, D), BF16),
-        xp=((ROWS, D), BF16),
         wx=((TP, nz, sh.xrows, HALF), BF16),
         gx=((TP, nz, sh.xrows, HALF), BF16),
         f1=((2, sh.fr, D), BF16),
@@ -146,7 +145,7 @@
         wf=((TP, nz, ny, br, D), BF16),
         wo=((2, nz, ny, br, HALF), BF16),
         par=((8, D), F32),
-        x=((ROWS, D), BF16),
+        both=((2, ROWS, D), BF16),
         gyt=((TP * TOKENS, D), BF16),
         gm=((2, 8, D), F32),
         qkv=((9, ROWS, 128), BF16),
@@ -159,7 +158,7 @@
         inv1=((OWN, 1), F32),
         h1b=((ROWS, D), BF16),
         gl=((2, ROWS, D), BF16),
-        sl=((2, ROWS, D), BF16),
+        ul=((2, ROWS, D), F32),
         fs=((OWN, D), BF16),
         fr=((OWN, D), BF16),
         n2=((OWN, D), F32),
@@ -246,6 +245,7 @@
     ssem, rsem, xsem, lsem = refs[-4:]
     count = len(names[0])
     b = types.SimpleNamespace(**dict(zip(names[0], refs[20 : 20 + count])))
+    b.xp, b.x = b.both.at[0], b.both.at[1]
     k = dict(zip(names[1], refs[20 + count : -4]))
     staged = [k[STAGED, i, 0] for i in range(12)]
     gmem, wq, wp, gain_in, bias_in, token_in, up_in, down_in = staged[:8]
@@ -617,25 +617,25 @@
         block = dot(b.turn[...], b.wx[:, :, :, cols].reshape(D, 128), TN).astype(BF16)
         b.wa[:, :, :, cols] = block.reshape(nz, ny, br, 128)
 
-    @pl.loop(0, 6)
+    @pl.loop(0, 2)
     def _(i):
-        @pl.when((i // 3) == seg)
-        def _():
-            forward_pair(i % 3)
-
-        @pl.when(i == 1)
-        def _():
-            for n in ("f2", "f0"):
-                gather_pass(n)
-
-        @pl.when((i == 2) & (seg == 1))
+        @pl.when((i == 1) & (seg == 1))
         def _():
             hops[0].wait_recv()
             b.x[256:272] = b.hopin[...]
-            b.xp[256:272] = dot(b.hopin[...], b.turn[...], NT).astype(BF16)
             rows = dot(b.hopin[...], attention_weight()).astype(BF16)
             for j in range(9):
                 b.qkv[j, 256:272] = rows[:, 128 * j : 128 * j + 128]
+
+        @pl.when(i == seg)
+        def _():
+            for p in range(3):
+                forward_pair(p)
+
+        @pl.when(i == 0)
+        def _():
+            for n in ("f2", "f0"):
+                gather_pass(n)
 
     def head_rows(ref, c):
         if nz > 1:
@@ -657,6 +657,11 @@
     b.inv1[...] = inv1
     b.h1b[own_rows] = h1.astype(BF16)
     h_swap = remote(b.h1b.at[own_rows], b.h1b.at[own_rows], sibling)
+
+    @pl.when(seg == 1)
+    def _():
+        b.xp[256:272] = dot(b.hopin[...], b.turn[...], NT).astype(BF16)
+
     for n in ("f1", "f2", "f0"):
         gather_done(n)
 
@@ -671,9 +676,8 @@
     def down_weight(t):
         return feed_weight(t, 1)
 
-    def activate(units):
-        erf = 0.5 * (1.0 + lax.erf(units * INV_ROOT_TWO))
-        return (units * erf).astype(BF16), erf
+    def gelu_share(units):
+        return 0.5 * (1.0 + lax.erf(units * INV_ROOT_TWO))
 
     early = pltpu.make_async_remote_copy(
         src_ref=b.es,
@@ -689,7 +693,8 @@
     def _():
         arrived([h_swap])
         rows = b.h1b[OWN + 256 : OWN + 272]
-        part = sum(dot(activate(dot(rows, up_weight(t)))[0], down_weight(t), NT) for t in range(2))
+        units = [dot(rows, up_weight(t)) for t in range(2)]
+        part = sum(dot((units[t] * gelu_share(units[t])).astype(BF16), down_weight(t), NT) for t in range(2))
 
         @pl.when(core == 0)
         def _():
@@ -708,9 +713,8 @@
     def project_up(rows):
         for t in range(2):
             units = dot(b.h1b[rows], up_weight(t))
-            active, erf = activate(units)
-            b.gl[t, rows] = active
-            b.sl[t, rows] = (erf + units * jnp.exp(-0.5 * units * units) * INV_ROOT_TWOPI).astype(BF16)
+            b.ul[t, rows] = units
+            b.gl[t, rows] = (units * gelu_share(units)).astype(BF16)
 
     @pl.loop(0, 2)
     def _(i):
@@ -845,23 +849,37 @@
             scatter_send(n, step + 1)
 
     down_names, up_names = ("t0", "t1", "t2"), ("i0", "i1", "i2")
-    def units_back(rows):
-        for t in range(2):
-            b.du[t, rows] = (dot(b.dfb[rows], down_weight(t)) * b.sl[t, rows].astype(F32)).astype(BF16)
-
-    units_back(own_rows)
     arrived([df_swap])
     weight_grad(b.gt, b.dfb, b.gl)
     for n in down_names:
         scatter_send(n, 0)
-    units_back(other_rows)
+    @pl.loop(0, 2)
+    def _(i):
+        rows = pl.ds(pl.multiple_of(OWN * i, 16), OWN)
+        for t in range(2):
+            units = b.ul[t, rows]
+            slope = gelu_share(units) + units * jnp.exp(-0.5 * units * units) * INV_ROOT_TWOPI
+            b.du[t, rows] = (dot(b.dfb[rows], down_weight(t)) * slope).astype(BF16)
+
 
     def partial_up(rows):
         return sum(dot(b.du[t, rows], up_weight(t), NT) for t in range(2))
 
-    b.dhs[...] = partial_up(other_rows).astype(BF16)
-    dh_swap = remote(b.dhs, b.dhr, sibling)
-    b.dz[...] = b.dz[...] + partial_up(own_rows)
+    dh_swap = Group(lambda: b.dhr)
+
+    @pl.loop(0, 2)
+    def _(i):
+        part = partial_up(pl.ds(pl.multiple_of(OWN * jnp.where(i == 0, other, core), 16), OWN))
+
+        @pl.when(i == 0)
+        def _():
+            b.dhs[...] = part.astype(BF16)
+            dh_swap.add(b.dhs, b.dhr, sibling)
+
+        @pl.when(i == 1)
+        def _():
+            b.dz[...] = b.dz[...] + part
+
     weight_grad(b.gi, b.h1b, b.du)
     for n in up_names:
         scatter_send(n, 0)
@@ -925,14 +943,16 @@
     def attention_grad(p):
         grads = jnp.concatenate([b.dqkv[3 * p + i] for i in range(3)], 1)
 
+        part = dot(b.both[jnp.minimum(p, 1)], grads, TN).astype(BF16)
+
         @pl.when(p == 0)
         def _():
-            b.gx[...] = dot(b.xp[...], grads, TN).astype(BF16).reshape(TP, nz, sh.xrows, HALF)
+            b.gx[...] = part.reshape(TP, nz, sh.xrows, HALF)
 
         @pl.when(p > 0)
         def _():
             cols = pl.ds(pl.multiple_of(HALF * p, 128), HALF)
-            b.ga[:, :, :, cols] = dot(b.x[...], grads, TN).astype(BF16).reshape(nz, ny, br, HALF)
+            b.ga[:, :, :, cols] = part.reshape(nz, ny, br, HALF)
 
     @pl.loop(0, 3)
     def _(p):

time: 118 us -> 118 us (level)
  no operation moved by 1% of the time
where the time goes in v1:
time: 118 us
  Pallas kernels  117 us (99%)
    pallas_call x1, Pallas kernels, layer(): pl.pallas_call(functools.partial(kernel, sh, names), name='layer', out_sh...  115 us

profile of v1, /device:TPU:1, one launch (start us, length us, event | category | flops | bytes accessed | tf_op | source)
XLA Modules:
  0.0 117.7 jit_solution(6222272479060335868)
XLA Ops:
  0.6 114.6 %layer.1 = (bf16[2,128,768]{2,1,0:T(8,128)(2,1)}, f32[2,8,768]{2,1,0:T(8,128)}, bf16[2,128,768]{2,1,0:T(8,128)(2,1)}, f32[2,8,1664]{2,1,0:T(8,128)}, f32[2,24,768]{2,1,0:T(8,128)}) custom-call(bf16[2,128,768]{2,1,0:T(8,128)(2,1)} %refs_0_.1, bf16[2,128,768]{2,1,0:T(8,128)(2,1)} %refs_1_.1, bf16[5,2,768]{2,1,0:T(2,128)(2,1)} %bitcast.7, ...), custom_call_target="tpu_custom_call" | custom-call | tf_op jit(solution)/shard_map/layer/pallas_call | solution.py:1100
  115.2 2.3 %unpack.1 = (bf16[2,128,768]{2,1,0:T(8,128)(2,1)}, bf16[5,2,768]{2,1,0:T(2,128)(2,1)}, f32[2,128,768]{2,1,0:T(8,128)}, f32[6,2304]{1,0:T(8,128)}, f32[6,768]{1,0...) custom-call(bf16[2,128,768]{2,1,0:T(8,128)(2,1)} %get-tuple-element., ...), custom_call_target="tpu_custom_call" | custom-call | tf_op jit(solution)/shard_map/unpack/pallas_call | solution.py:1179

commit v2 on v1

--- a/solution.py
+++ b/solution.py
@@ -221,7 +221,7 @@
     jobs.append(("a1", zy, slice(HALF, 2 * HALF), zy))
     jobs.append(("a2", yz, slice(2 * HALF, 2 * HALF + 256), zy))
     jobs.append(("a3", zy, slice(2 * HALF + 256, 3 * HALF), zy))
-    jobs.append(("as", zy, slice(4 * HALF, ACOLS), zy))
+    jobs.append(("as", yz, slice(4 * HALF, ACOLS), zy))
     return jobs
 
 
@@ -761,12 +761,22 @@
     b.dfb[own_rows] = dz.astype(BF16)
     df_swap = remote(b.dfb.at[own_rows], b.dfb.at[own_rows], sibling)
 
-    def weight_grad(into, left, right):
+    def weight_grad(into, left, right, jobs_):
         @pl.loop(0, 2)
         def _(t):
             part = dot(left[...], right[t], TN).astype(BF16)
             for i in range(2):
                 into[2 * t + i] = part[:, HALF * i : HALF * (i + 1)].reshape(nz, ny, br, HALF)
+
+            for h in range(2):
+
+                @pl.when(t == h)
+                def _():
+                    for n in jobs_:
+                        if is_ring(n, 0) and scatters[n][1][0] != "x":
+                            ring_send(n, h)
+                        elif h == 1:
+                            scatter_send(n, 0)
 
     scatters = {j[0]: j for j in scatter_jobs()}
     rs = {}
@@ -796,24 +806,30 @@
 
         return part
 
+    def ring_send(name, half):
+        axis = scatters[name][1][0]
+        n = size[axis]
+        part = source_of(name, 0)
+        landing, over = k[LANDED, 0, name], k[PASSED, 0, name]
+        right, left, far = (near[axis][o] for o in (1, n - 1, 2))
+        to = moved(axis, 1), moved(axis, n - 1)
+        cut = size[[a for a in scatters[name][3] if a != axis][0]] // 2
+        if name not in rs:
+            rs[name] = ([None, None], Group(lambda: landing), cut, (right, left), to)
+        rs[name][0][half] = remote(part(far, half), lambda: over.at[half], to[half])
+        if half == 0:
+            rs[name][1].add(part(left, 0), landing.at[1, :cut], to[1])
+        else:
+            rs[name][1].add(part(right, 1), landing.at[0, cut:], to[0])
+
     def scatter_send(name, step):
         axis = scatters[name][1][step]
         n = size[axis]
         part = source_of(name, step)
         landing = k[LANDED, step, name]
         if is_ring(name, step):
-            right, left, far = (near[axis][o] for o in (1, n - 1, 2))
-            to_right, to_left = moved(axis, 1), moved(axis, n - 1)
-            half = size[[a for a in scatters[name][3] if a != axis][0]] // 2
-            over = k[PASSED, 0, name]
-            passing = [
-                remote(part(far, 0), lambda: over.at[0], to_right),
-                remote(part(far, 1), lambda: over.at[1], to_left),
-            ]
-            coming = Group(lambda: landing)
-            coming.add(part(right, 1), landing.at[0, half:], to_right)
-            coming.add(part(left, 0), landing.at[1, :half], to_left)
-            rs[name] = (passing, coming, half, (right, left), (to_right, to_left))
+            ring_send(name, 0)
+            ring_send(name, 1)
             return
         rs[name] = [Group(lambda: landing)] if n > 1 else []
         for o in range(1, n):
@@ -850,9 +866,7 @@
 
     down_names, up_names = ("t0", "t1", "t2"), ("i0", "i1", "i2")
     arrived([df_swap])
-    weight_grad(b.gt, b.dfb, b.gl)
-    for n in down_names:
-        scatter_send(n, 0)
+    weight_grad(b.gt, b.dfb, b.gl, down_names)
     @pl.loop(0, 2)
     def _(i):
         rows = pl.ds(pl.multiple_of(OWN * i, 16), OWN)
@@ -861,6 +875,9 @@
             slope = gelu_share(units) + units * jnp.exp(-0.5 * units * units) * INV_ROOT_TWOPI
             b.du[t, rows] = (dot(b.dfb[rows], down_weight(t)) * slope).astype(BF16)
 
+    weight_grad(b.gi, b.h1b, b.du, up_names)
+    for n in down_names:
+        scatter_pass(n)
 
     def partial_up(rows):
         return sum(dot(b.du[t, rows], up_weight(t), NT) for t in range(2))
@@ -880,11 +897,6 @@
         def _():
             b.dz[...] = b.dz[...] + part
 
-    weight_grad(b.gi, b.h1b, b.du)
-    for n in up_names:
-        scatter_send(n, 0)
-    for n in down_names:
-        scatter_pass(n)
     arrived([dh_swap])
     into_first = b.dz[...] + b.dhr[...].astype(F32)
     b.sg[0:1] = column_sum(into_first * b.n1[...])
@@ -964,11 +976,11 @@
             arrived([go_swap])
             scatter_send("aw", 0)
             scatter_send("x0", 0)
-
-        @pl.when(p == 1)
-        def _():
             for n in up_names:
                 scatter_pass(n)
+
+        @pl.when(p == 1)
+        def _():
             scatter_send("a1", 0)
             scatter_on(down_names, 0)
             for n in ("aw", "x0"):
@@ -979,6 +991,7 @@
             scatter_send("a2", 0)
             scatter_send("a3", 0)
             scatter_pass("a1")
+            scatter_on(up_names, 0)
 
 
     def partial_input(rows):
@@ -1012,7 +1025,6 @@
     b.ga[:, :, :, 4 * HALF :] = small_grads.reshape(nz, ny, br, SMALL)
     scatter_send("as", 0)
     attention_names = ("aw", "x0", "a1", "a2", "a3", "as")
-    scatter_on(up_names, 0)
     scatter_on(down_names, 1)
     scatter_on(attention_names, 0)
     scatter_on(up_names, 1)

time: 118 us -> 118 us (level)
  no operation moved by 1% of the time
where the time goes in v2:
time: 118 us
  Pallas kernels  117 us (99%)
    pallas_call x1, Pallas kernels, layer(): pl.pallas_call(functools.partial(kernel, sh, names), name='layer', out_sh...  115 us

profile of v2, /device:TPU:1, one launch (start us, length us, event | category | flops | bytes accessed | tf_op | source)
XLA Modules:
  0.0 118.1 jit_solution(9197346939844755925)
XLA Ops:
  0.6 115.0 %layer.1 = (bf16[2,128,768]{2,1,0:T(8,128)(2,1)}, f32[2,8,768]{2,1,0:T(8,128)}, bf16[2,128,768]{2,1,0:T(8,128)(2,1)}, f32[2,8,1664]{2,1,0:T(8,128)}, f32[2,24,768]{2,1,0:T(8,128)}) custom-call(bf16[2,128,768]{2,1,0:T(8,128)(2,1)} %refs_0_.1, bf16[2,128,768]{2,1,0:T(8,128)(2,1)} %refs_1_.1, bf16[5,2,768]{2,1,0:T(2,128)(2,1)} %bitcast.7, ...), custom_call_target="tpu_custom_call" | custom-call | tf_op jit(solution)/shard_map/layer/pallas_call | solution.py:1112
  115.6 2.3 %unpack.1 = (bf16[2,128,768]{2,1,0:T(8,128)(2,1)}, bf16[5,2,768]{2,1,0:T(2,128)(2,1)}, f32[2,128,768]{2,1,0:T(8,128)}, f32[6,2304]{1,0:T(8,128)}, f32[6,768]{1,0...) custom-call(bf16[2,128,768]{2,1,0:T(8,128)(2,1)} %get-tuple-element., ...), custom_call_target="tpu_custom_call" | custom-call | tf_op jit(solution)/shard_map/unpack/pallas_call | solution.py:1191

commit v3 on v2

--- a/solution.py
+++ b/solution.py
@@ -184,6 +184,9 @@
         dxr=((OWN, D), BF16),
         dxb=((TP * TOKENS, D), BF16),
         sg=((48, D), F32),
+        ms=((16, D), F32),
+        mr=((16, D), F32),
+        tot=((br, REST), BF16),
         e3=((TP, 2 * sh.pc, REST), BF16),
         r3=((TP - 1, 2 * sh.pc, REST), BF16),
         e3y=((ny, 2 * sh.pc, HALF), BF16),
@@ -875,9 +878,6 @@
             slope = gelu_share(units) + units * jnp.exp(-0.5 * units * units) * INV_ROOT_TWOPI
             b.du[t, rows] = (dot(b.dfb[rows], down_weight(t)) * slope).astype(BF16)
 
-    weight_grad(b.gi, b.h1b, b.du, up_names)
-    for n in down_names:
-        scatter_pass(n)
 
     def partial_up(rows):
         return sum(dot(b.du[t, rows], up_weight(t), NT) for t in range(2))
@@ -911,9 +911,11 @@
         for p in range(3):
             b.doc[p, rows] = (parts[0] + parts[1])[:, 128 * p : 128 * p + 128].astype(BF16)
 
-    grad_mixed(own_rows)
+    weight_grad(b.gi, b.h1b, b.du, up_names)
+    for n in down_names:
+        scatter_pass(n)
     arrived([da_swap])
-    grad_mixed(other_rows)
+    grad_mixed(slice(None))
 
     mixed_t = b.ot[...].reshape(HALF, ROWS)
 
@@ -991,15 +993,33 @@
             scatter_send("a2", 0)
             scatter_send("a3", 0)
             scatter_pass("a1")
-            scatter_on(up_names, 0)
 
 
     def partial_input(rows):
         return dot(joined(rows, range(9)), attention_weight(), NT)
 
+    memory_rows = [pl.ds(pl.multiple_of(OWN * c + 256, 16), 16) for c in (other, core)]
+    part = dot(jnp.concatenate([joined(rows, range(9)) for rows in memory_rows], 0), attention_weight(), NT)
+    b.ms[...] = part[:16]
+    memory_swap = remote(b.ms, b.mr, sibling)
     b.dxs[...] = partial_input(other_rows).astype(BF16)
     dx_swap = remote(b.dxs, b.dxr, sibling)
+    arrived([memory_swap])
+    memory_grad = part[16:] + b.dr[256:272] + b.mr[...]
+
+    @pl.when((core == 0) & (seg == 0))
+    def _():
+        b.sg[16:32] = memory_grad
+
+    @pl.when(core == 1)
+    def _():
+        b.sg[32:48] = memory_grad
+
+    small_grads = dot(b.sg[...].astype(BF16), smallsel[...], TN).astype(BF16)
+    b.ga[:, :, :, 4 * HALF :] = small_grads.reshape(nz, ny, br, SMALL)
+    scatter_send("as", 0)
     dx = partial_input(own_rows) + b.dr[...]
+    scatter_on(up_names, 0)
     arrived([dx_swap])
     dx = dx + b.dxr[...].astype(F32)
     b.dxb[...] = dx[:256].astype(BF16)
@@ -1012,45 +1032,31 @@
             5,
             i,
         )
-
-    @pl.when((core == 0) & (seg == 0))
-    def _():
-        b.sg[16:32] = dx[256:272]
-
-    @pl.when(core == 1)
-    def _():
-        b.sg[32:48] = dx[256:272]
-
-    small_grads = dot(b.sg[...].astype(BF16), smallsel[...], TN).astype(BF16)
-    b.ga[:, :, :, 4 * HALF :] = small_grads.reshape(nz, ny, br, SMALL)
-    scatter_send("as", 0)
-    attention_names = ("aw", "x0", "a1", "a2", "a3", "as")
+    scatter_on(("aw", "x0", "a1"), 0)
     scatter_on(down_names, 1)
-    scatter_on(attention_names, 0)
+    scatter_on(("a2", "a3", "as"), 0)
+    spread = dot(packy[...], scatter_sum("x0", 1).astype(BF16), TN).astype(BF16)
+    b.e3y[...] = spread.reshape(ny, 2 * sh.pc, HALF)
+    ysteps = [Group(lambda: b.r3y)] if ny > 1 else []
+    for o in range(1, ny):
+        ysteps[0].add(b.e3y.at[near["y"][o]], b.r3y.at[o - 1], moved("y", o))
     scatter_on(up_names, 1)
-
-    def last_rows(names, first_col):
-        for j, n in enumerate(names):
+    for n in ("aw", "a1", "a2", "a3", "as"):
+        cols = scatters[n][2]
+        b.tot[:, cols.start - HALF : cols.stop - HALF] = scatter_sum(n, 1).astype(BF16)
+    spread = dot(packsel[...], b.tot[...], TN).astype(BF16)
+    b.e3[...] = spread.reshape(TP, 2 * sh.pc, REST)
+    steps = [Group(lambda: b.r3)]
+    for o in range(1, TP):
+        steps[0].add(b.e3.at[near["x"][o]], b.r3.at[o - 1], moved("x", o))
+
+    def last_rows(wanted, first_col):
+        for j, n in enumerate(wanted):
             total = scatter_sum(n, 2)
             cols = slice(first_col + 128 * j, first_col + 128 * j + 128)
             b.sf[0, :, cols] = total[:wr]
             b.sf[1, :, cols] = total[wr:]
 
-    for n in attention_names:
-        cols = scatters[n][2]
-        total = scatter_sum(n, 1).astype(BF16)
-        if n == "x0":
-            spread = dot(packy[...], total, TN).astype(BF16)
-            b.e3y[...] = spread.reshape(ny, 2 * sh.pc, HALF)
-            ysteps = [Group(lambda: b.r3y)] if ny > 1 else []
-            for o in range(1, ny):
-                ysteps[0].add(b.e3y.at[(y + o) % ny], b.r3y.at[o - 1], moved("y", o))
-        else:
-            spread = dot(packsel[...], total, TN).astype(BF16)
-            b.e3[:, :, cols.start - HALF : cols.stop - HALF] = spread.reshape(TP, 2 * sh.pc, cols.stop - cols.start)
-    steps = [Group(lambda: b.r3)]
-    for o in range(1, TP):
-        steps[0].add(b.e3.at[(x + o) % TP], b.r3.at[o - 1], moved("x", o))
     last_rows(down_names, HALF)
     last_rows(up_names, 0)
     sf_local = local(b.sf.at[core], gfo.at[core])

time: 118 us -> 116 us (0.983)
  Pallas kernels: 117 us -> 115 us
    pallas_call x1, Pallas kernels: 115 us -> 112 us  [layer(): pl.pallas_call(functools.partial(kernel, sh, names), name='layer', out_sh...]
where the time goes in v3:
time: 116 us; the launch traced here: 115 us
  Pallas kernels  115 us (99%)
    pallas_call x1, Pallas kernels, layer(): pl.pallas_call(functools.partial(kernel, sh, names), name='layer', out_sh...  112 us

profile of v3, /device:TPU:1, one launch (start us, length us, event | category | flops | bytes accessed | tf_op | source)
XLA Modules:
  0.0 115.4 jit_solution(8538479276854298945)
XLA Ops:
  0.6 112.3 %layer.1 = (bf16[2,128,768]{2,1,0:T(8,128)(2,1)}, f32[2,8,768]{2,1,0:T(8,128)}, bf16[2,128,768]{2,1,0:T(8,128)(2,1)}, f32[2,8,1664]{2,1,0:T(8,128)}, f32[2,24,768]{2,1,0:T(8,128)}) custom-call(bf16[2,128,768]{2,1,0:T(8,128)(2,1)} %refs_0_.1, bf16[2,128,768]{2,1,0:T(8,128)(2,1)} %refs_1_.1, bf16[5,2,768]{2,1,0:T(2,128)(2,1)} %bitcast.7, ...), custom_call_target="tpu_custom_call" | custom-call | tf_op jit(solution)/shard_map/layer/pallas_call | solution.py:1118
  113.0 2.3 %unpack.1 = (bf16[2,128,768]{2,1,0:T(8,128)(2,1)}, bf16[5,2,768]{2,1,0:T(2,128)(2,1)}, f32[2,128,768]{2,1,0:T(8,128)}, f32[6,2304]{1,0:T(8,128)}, f32[6,768]{1,0...) custom-call(bf16[2,128,768]{2,1,0:T(8,128)(2,1)} %get-tuple-element., ...), custom_call_target="tpu_custom_call" | custom-call | tf_op jit(solution)/shard_map/unpack/pallas_call | solution.py:1197

commit v4 on v3

--- a/solution.py
+++ b/solution.py
@@ -978,21 +978,20 @@
             arrived([go_swap])
             scatter_send("aw", 0)
             scatter_send("x0", 0)
+
+        @pl.when(p == 1)
+        def _():
+            scatter_send("a1", 0)
             for n in up_names:
                 scatter_pass(n)
 
-        @pl.when(p == 1)
-        def _():
-            scatter_send("a1", 0)
-            scatter_on(down_names, 0)
+        @pl.when(p == 2)
+        def _():
+            scatter_send("a2", 0)
+            scatter_send("a3", 0)
             for n in ("aw", "x0"):
                 scatter_pass(n)
-
-        @pl.when(p == 2)
-        def _():
-            scatter_send("a2", 0)
-            scatter_send("a3", 0)
-            scatter_pass("a1")
+            scatter_on(down_names, 0)
 
 
     def partial_input(rows):
@@ -1018,6 +1017,7 @@
     small_grads = dot(b.sg[...].astype(BF16), smallsel[...], TN).astype(BF16)
     b.ga[:, :, :, 4 * HALF :] = small_grads.reshape(nz, ny, br, SMALL)
     scatter_send("as", 0)
+    scatter_pass("a1")
     dx = partial_input(own_rows) + b.dr[...]
     scatter_on(up_names, 0)
     arrived([dx_swap])

time: 116 us -> 115 us (level)
  no operation moved by 1% of the time
where the time goes in v4:
time: 115 us
  Pallas kernels  114 us (99%)
    pallas_call x1, Pallas kernels, layer(): pl.pallas_call(functools.partial(kernel, sh, names), name='layer', out_sh...  112 us

profile of v4, /device:TPU:1, one launch (start us, length us, event | category | flops | bytes accessed | tf_op | source)
XLA Modules:
  0.0 114.9 jit_solution(14778980074432025839)
XLA Ops:
  0.6 111.8 %layer.1 = (bf16[2,128,768]{2,1,0:T(8,128)(2,1)}, f32[2,8,768]{2,1,0:T(8,128)}, bf16[2,128,768]{2,1,0:T(8,128)(2,1)}, f32[2,8,1664]{2,1,0:T(8,128)}, f32[2,24,768]{2,1,0:T(8,128)}) custom-call(bf16[2,128,768]{2,1,0:T(8,128)(2,1)} %refs_0_.1, bf16[2,128,768]{2,1,0:T(8,128)(2,1)} %refs_1_.1, bf16[5,2,768]{2,1,0:T(2,128)(2,1)} %bitcast.7, ...), custom_call_target="tpu_custom_call" | custom-call | tf_op jit(solution)/shard_map/layer/pallas_call | solution.py:1118
  112.4 2.3 %unpack.1 = (bf16[2,128,768]{2,1,0:T(8,128)(2,1)}, bf16[5,2,768]{2,1,0:T(2,128)(2,1)}, f32[2,128,768]{2,1,0:T(8,128)}, f32[6,2304]{1,0:T(8,128)}, f32[6,768]{1,0...) custom-call(bf16[2,128,768]{2,1,0:T(8,128)(2,1)} %get-tuple-element., ...), custom_call_target="tpu_custom_call" | custom-call | tf_op jit(solution)/shard_map/unpack/pallas_call | solution.py:1197

commit v5 on v4

--- a/solution.py
+++ b/solution.py
@@ -186,9 +186,13 @@
         sg=((48, D), F32),
         ms=((16, D), F32),
         mr=((16, D), F32),
-        tot=((br, REST), BF16),
-        e3=((TP, 2 * sh.pc, REST), BF16),
-        r3=((TP - 1, 2 * sh.pc, REST), BF16),
+        tot=((br, 2 * HALF), BF16),
+        e3=((TP, 2 * sh.pc, 2 * HALF), BF16),
+        r3=((TP - 1, 2 * sh.pc, 2 * HALF), BF16),
+        ez=((nz, TP, 2 * sh.pc, 256), BF16),
+        rz=((nz * TP - 1, 2 * sh.pc, 256), BF16),
+        ey=((ny, TP, 2 * sh.pc, 256), BF16),
+        ry=((ny * TP - 1, 2 * sh.pc, 256), BF16),
         e3y=((ny, 2 * sh.pc, HALF), BF16),
         r3y=((max(1, ny - 1), 2 * sh.pc, HALF), BF16),
         s4=((2, sh.pc, ACOLS), F32),
@@ -224,7 +228,7 @@
     jobs.append(("a1", zy, slice(HALF, 2 * HALF), zy))
     jobs.append(("a2", yz, slice(2 * HALF, 2 * HALF + 256), zy))
     jobs.append(("a3", zy, slice(2 * HALF + 256, 3 * HALF), zy))
-    jobs.append(("as", yz, slice(4 * HALF, ACOLS), zy))
+    jobs.append(("as", zy, slice(4 * HALF, ACOLS), zy))
     return jobs
 
 
@@ -278,6 +282,11 @@
         there[axis] = near[axis][offset]
         return device(there["x"], there["y"], there["z"], core_)
 
+    def plane_device(axis, offset, x_offset):
+        there = dict(at)
+        there[axis], there["x"] = near[axis][offset], near["x"][x_offset]
+        return device(there["x"], there["y"], there["z"])
+
     neighbours = {a: [moved_to(a, o) for o in range(size[a])] for a in at}
 
     def moved(axis, offset):
@@ -340,6 +349,7 @@
     for axis in ("y", "z"):
         for o in range(1, size[axis]):
             peers.append(moved(axis, o))
+            peers += [plane_device(axis, o, o2) for o2 in range(1, TP)]
     for peer in peers:
         pl.semaphore_signal(barrier, inc=1, device_id=peer, device_id_type=MESH)
 
@@ -1034,21 +1044,45 @@
         )
     scatter_on(("aw", "x0", "a1"), 0)
     scatter_on(down_names, 1)
-    scatter_on(("a2", "a3", "as"), 0)
+
+    def plane_send(axis, wanted, spread_, landed):
+        n = size[axis]
+        for name in wanted:
+            scatter_sum(name, 0)
+        rows = jnp.concatenate([k[SUMMED, 0, name][i] for i in range(n) for name in wanted], 1)
+        part = dot(packsel[...], rows, TN).astype(BF16)
+        for i in range(n):
+            spread_[i] = part[:, 256 * i : 256 * (i + 1)].reshape(TP, 2 * sh.pc, 256)
+        group = Group(lambda: landed)
+        for o in range(n):
+            for o2 in range(TP):
+                if o + o2 > 0:
+                    source = spread_.at[near[axis][o], near["x"][o2]]
+                    group.add(source, landed.at[o * TP + o2 - 1], plane_device(axis, o, o2))
+        return group
+
+    def plane_total(axis, spread_, landed, group):
+        arrived([group])
+        total = spread_[at[axis], x].astype(F32)
+        for i in range(size[axis] * TP - 1):
+            total = total + landed[i].astype(F32)
+        return total.reshape(2, sh.pc, 256)
+
+    plane_z = plane_send("z", ("a2",), b.ez, b.rz)
+    plane_y = plane_send("y", ("a3", "as"), b.ey, b.ry)
     spread = dot(packy[...], scatter_sum("x0", 1).astype(BF16), TN).astype(BF16)
     b.e3y[...] = spread.reshape(ny, 2 * sh.pc, HALF)
     ysteps = [Group(lambda: b.r3y)] if ny > 1 else []
     for o in range(1, ny):
         ysteps[0].add(b.e3y.at[near["y"][o]], b.r3y.at[o - 1], moved("y", o))
-    scatter_on(up_names, 1)
-    for n in ("aw", "a1", "a2", "a3", "as"):
-        cols = scatters[n][2]
-        b.tot[:, cols.start - HALF : cols.stop - HALF] = scatter_sum(n, 1).astype(BF16)
+    for i, n in enumerate(("a1", "aw")):
+        b.tot[:, HALF * i : HALF * (i + 1)] = scatter_sum(n, 1).astype(BF16)
     spread = dot(packsel[...], b.tot[...], TN).astype(BF16)
-    b.e3[...] = spread.reshape(TP, 2 * sh.pc, REST)
+    b.e3[...] = spread.reshape(TP, 2 * sh.pc, 2 * HALF)
     steps = [Group(lambda: b.r3)]
     for o in range(1, TP):
         steps[0].add(b.e3.at[near["x"][o]], b.r3.at[o - 1], moved("x", o))
+    scatter_on(up_names, 1)
 
     def last_rows(wanted, first_col):
         for j, n in enumerate(wanted):
@@ -1066,12 +1100,18 @@
     total = b.e3[x].astype(F32)
     for o in range(1, TP):
         total = total + b.r3[o - 1].astype(F32)
-    b.s4[:, :, HALF:] = total.reshape(2, sh.pc, REST)
+    total = total.reshape(2, sh.pc, 2 * HALF)
+    b.s4[:, :, HALF : 2 * HALF] = total[:, :, :HALF]
+    b.s4[:, :, WO : WO + HALF] = total[:, :, HALF:]
     arrived(ysteps)
     total = b.e3y[y].astype(F32)
     for o in range(1, ny):
         total = total + b.r3y[o - 1].astype(F32)
     b.s4[:, :, :HALF] = total.reshape(2, sh.pc, HALF)
+    b.s4[:, :, 2 * HALF : 2 * HALF + 256] = plane_total("z", b.ez, b.rz, plane_z)
+    total = plane_total("y", b.ey, b.ry, plane_y)
+    b.s4[:, :, 2 * HALF + 256 : 3 * HALF] = total[:, :, :128]
+    b.s4[:, :, 4 * HALF :] = total[:, :, 128:]
     s4_local = local(b.s4.at[core], gao.at[core])
     s4_swap = remote(b.s4.at[other], gao.at[core], sibling)
 

time: 115 us -> 118 us (1.026)
  Pallas kernels: 114 us -> 117 us
    pallas_call x1, Pallas kernels: 112 us -> 115 us  [layer(): pl.pallas_call(functools.partial(kernel, sh, names), name='layer', out_sh...]
where the time goes in v5:
time: 118 us
  Pallas kernels  117 us (99%)
    pallas_call x1, Pallas kernels, layer(): pl.pallas_call(functools.partial(kernel, sh, names), name='layer', out_sh...  115 us

profile of v5, /device:TPU:1, one launch (start us, length us, event | category | flops | bytes accessed | tf_op | source)
XLA Modules:
  0.0 118.2 jit_solution(3240335266034714577)
XLA Ops:
  0.6 115.1 %layer.1 = (bf16[2,128,768]{2,1,0:T(8,128)(2,1)}, f32[2,8,768]{2,1,0:T(8,128)}, bf16[2,128,768]{2,1,0:T(8,128)(2,1)}, f32[2,8,1664]{2,1,0:T(8,128)}, f32[2,24,768]{2,1,0:T(8,128)}) custom-call(bf16[2,128,768]{2,1,0:T(8,128)(2,1)} %refs_0_.1, bf16[2,128,768]{2,1,0:T(8,128)(2,1)} %refs_1_.1, bf16[5,2,768]{2,1,0:T(2,128)(2,1)} %bitcast.7, ...), custom_call_target="tpu_custom_call" | custom-call | tf_op jit(solution)/shard_map/layer/pallas_call | solution.py:1158
  115.8 2.3 %unpack.1 = (bf16[2,128,768]{2,1,0:T(8,128)(2,1)}, bf16[5,2,768]{2,1,0:T(2,128)(2,1)}, f32[2,128,768]{2,1,0:T(8,128)}, f32[6,2304]{1,0:T(8,128)}, f32[6,768]{1,0...) custom-call(bf16[2,128,768]{2,1,0:T(8,128)(2,1)} %get-tuple-element., ...), custom_call_target="tpu_custom_call" | custom-call | tf_op jit(solution)/shard_map/unpack/pallas_call | solution.py:1237

commit v6 on v4

--- a/solution.py
+++ b/solution.py
@@ -510,10 +510,10 @@
     b.wa[z, y, :, HALF:] = dot(packsel[...], b.p2[...].reshape(TP * 2 * sh.pc, REST)).astype(BF16)
     for n in ("a0", "a1"):
         gather_start(n, 0)
-    for n in feed_names:
+    for n in first_names:
         gather_done(n)
         gather_start(n, 1)
-    for n in first_names:
+    for n in feed_names:
         gather_done(n)
         gather_start(n, 1)
     for n in first_names:

time: 115 us -> 120 us (1.043)
  Pallas kernels: 114 us -> 119 us
    pallas_call x1, Pallas kernels: 112 us -> 117 us  [layer(): pl.pallas_call(functools.partial(kernel, sh, names), name='layer', out_sh...]
where the time goes in v6:
time: 120 us
  Pallas kernels  119 us (99%)
    pallas_call x1, Pallas kernels, layer(): pl.pallas_call(functools.partial(kernel, sh, names), name='layer', out_sh...  117 us

profile of v6, /device:TPU:1, one launch (start us, length us, event | category | flops | bytes accessed | tf_op | source)
XLA Modules:
  0.0 119.7 jit_solution(14928009483825279192)
XLA Ops:
  0.6 116.6 %layer.1 = (bf16[2,128,768]{2,1,0:T(8,128)(2,1)}, f32[2,8,768]{2,1,0:T(8,128)}, bf16[2,128,768]{2,1,0:T(8,128)(2,1)}, f32[2,8,1664]{2,1,0:T(8,128)}, f32[2,24,768]{2,1,0:T(8,128)}) custom-call(bf16[2,128,768]{2,1,0:T(8,128)(2,1)} %refs_0_.1, bf16[2,128,768]{2,1,0:T(8,128)(2,1)} %refs_1_.1, bf16[5,2,768]{2,1,0:T(2,128)(2,1)} %bitcast.7, ...), custom_call_target="tpu_custom_call" | custom-call | tf_op jit(solution)/shard_map/layer/pallas_call | solution.py:1118
  117.2 2.3 %unpack.1 = (bf16[2,128,768]{2,1,0:T(8,128)(2,1)}, bf16[5,2,768]{2,1,0:T(2,128)(2,1)}, f32[2,128,768]{2,1,0:T(8,128)}, f32[6,2304]{1,0:T(8,128)}, f32[6,768]{1,0...) custom-call(bf16[2,128,768]{2,1,0:T(8,128)(2,1)} %get-tuple-element., ...), custom_call_target="tpu_custom_call" | custom-call | tf_op jit(solution)/shard_map/unpack/pallas_call | solution.py:1197
